TPU v7x, 32 devices: a whole 2x2x4 slice. The times are simulated.
32 devices in a mesh: dp: 8 (over z, core), tensor: 4 (over y, x).
Axes of the slice: x: 2, y: 2, z: 4, core: 2. Of those that a mesh axis runs over, the one named last changes fastest.
Arguments:
- attention: bfloat16 [4096, 4096], P('dp', 'tensor'), may hold values from -6 to 6
- code_blocks: bfloat16 [4096, 4096], P('tensor'), may hold values from -4 to 4
- block_scales: float32 [32, 32], P('tensor'), may hold values from 0.008 to 0.032
- residual: bfloat16 [4096, 4096], P('dp', 'tensor'), may hold values from -6 to 6
- low_feature: bfloat16 [4096, 4096], P('dp', 'tensor'), may hold values from -6 to 6
- mid_feature: bfloat16 [4096, 4096], P('dp', 'tensor'), may hold values from -6 to 6
- join_weight: bfloat16 [4096, 3, 4096], P('dp', None, 'tensor'), may hold values from -0.0546875 to 0.0546875
- draft_gain: float32 [3, 4096], replicated, may hold values from 0.5 to 2
- cotangent: bfloat16 [3, 4096, 4096], P(None, ('dp', 'tensor')), may hold values from -6 to 6
- loss_mask: int32 [4096], P(('dp', 'tensor')), may hold values 0 or 1
Outputs:
- grad_join: float32 [4096, 3, 4096], P('dp', None, 'tensor')
- grad_gain: float32 [3, 4096], replicated
All inputs are finite; a program needn't handle non-finite values. No bound on the sum of `loss_mask` on one device may be relied on, other than what follows from the above.
Results may differ from a plain program's by a relative error of at most 0.023.
Values may be sent and summed in bfloat16 or wider, within the bound.
A program may use at most 128 MiB of HBM per device.

v0:
```python
import jax
import jax.numpy as jnp
from jax import lax
from jax.sharding import PartitionSpec as P

BLOCK = 128
STEPS = 3
PARTS = 2


EPS = 1e-05


def project_heads(attention, code_blocks, block_scales, shares):
    heads, features = code_blocks.shape
    scales = jnp.repeat(block_scales, BLOCK, axis=1)[:, None, :]
    weights = code_blocks.reshape(-1, BLOCK, features).astype(jnp.float32) * scales
    weights = lax.optimization_barrier(weights.astype(jnp.bfloat16).reshape(heads, features))
    own = features // shares
    return jnp.stack(
        [
            jnp.dot(
                attention,
                weights[:, share * own : (share + 1) * own],
                preferred_element_type=jnp.float32,
            ).astype(jnp.bfloat16)
            for share in range(shares)
        ]
    )


def draft_loss(joined_sum, gain_table, cotangent, token_mask, loss_scale):
    current = joined_sum
    running = jnp.zeros((), jnp.float32)
    keeper = token_mask.astype(jnp.float32)[:, None]
    for step_index in range(STEPS):
        square_mean = jnp.mean(current * current, axis=-1, keepdims=True)
        normed = current * lax.rsqrt(square_mean + EPS) * gain_table[step_index][None, :]
        current = current + jax.nn.silu(normed)
        running = running + jnp.sum(keeper * cotangent[step_index].astype(jnp.float32) * current)
    return running * loss_scale


def on_device(
    attention,
    code_blocks,
    block_scales,
    residual,
    low_feature,
    mid_feature,
    join_weight,
    draft_gain,
    cotangent,
    loss_mask,
):
    n_dp = lax.axis_size("dp")
    n_tensor = lax.axis_size("tensor")
    tok_dev, width = residual.shape
    own_tokens = loss_mask.shape[0]
    rows = own_tokens // PARTS
    own_out = join_weight.shape[0]
    loss_scale = float(tok_dev * n_dp) ** (-0.5)

    def piece(feature, part):
        grouped = feature.reshape(n_tensor, PARTS, rows, -1)[:, part]
        return grouped.reshape(n_tensor * rows, -1)

    def gathered(own_piece):
        return lax.all_gather(own_piece, "dp", axis=0, tiled=True)

    outer = jnp.concatenate([low_feature, mid_feature], axis=1)
    outer_all = [gathered(piece(outer, part)) for part in range(PARTS)]
    partial_value = project_heads(attention, code_blocks, block_scales, n_tensor)
    own_share = lax.psum_scatter(partial_value, "tensor", scatter_dimension=0, tiled=False)
    high_feature = (residual.astype(jnp.float32) + own_share.astype(jnp.float32)).astype(jnp.bfloat16)
    high_feature, outer_all[0] = lax.optimization_barrier((high_feature, outer_all[0]))
    high_all = [gathered(piece(high_feature, part)) for part in range(PARTS)]

    outer_weight = join_weight[:, :2].reshape(own_out, -1)
    high_weight = join_weight[:, 2]
    gain_grad = jnp.zeros(draft_gain.shape, jnp.float32)
    outer_grad = jnp.zeros((own_out, 2 * width), jnp.float32)
    high_grad = jnp.zeros((own_out, width), jnp.float32)
    joined_own = grad_own = None
    high_all[0], *outer_all = lax.optimization_barrier((high_all[0], *outer_all))
    for part in range(PARTS):
        if part > 0:
            high_all[part], joined_own = lax.optimization_barrier((high_all[part], joined_own))
        joined_partial = jnp.dot(
            outer_all[part], outer_weight.T, preferred_element_type=jnp.float32
        ) + jnp.dot(high_all[part], high_weight.T, preferred_element_type=jnp.float32)
        joined_partial = joined_partial.astype(jnp.bfloat16).reshape(n_dp, n_tensor, rows, own_out)
        scattered = lax.psum_scatter(
            joined_partial.transpose(1, 0, 2, 3), "tensor", scatter_dimension=0, tiled=False
        )
        if part > 0:
            scattered, grad_own = lax.optimization_barrier((scattered, grad_own))
        joined_own = lax.all_to_all(scattered, "dp", split_axis=0, concat_axis=0, tiled=True)
        joined_sum = joined_own.transpose(1, 0, 2).reshape(rows, -1).astype(jnp.float32)
        lower = part * rows
        joined_grad, part_gain = jax.grad(draft_loss, argnums=(0, 1))(
            joined_sum,
            draft_gain,
            cotangent[:, lower : lower + rows],
            loss_mask[lower : lower + rows],
            loss_scale,
        )
        gain_grad = gain_grad + part_gain
        grad_own = joined_grad.astype(jnp.bfloat16).reshape(rows, n_dp, own_out).transpose(1, 0, 2)
        grad_own = lax.all_to_all(grad_own, "dp", split_axis=0, concat_axis=0, tiled=True)
        if part == PARTS - 1:
            gain_grad, grad_own = lax.optimization_barrier((gain_grad, grad_own))
        grad_all = lax.all_gather(grad_own, "tensor", axis=0, tiled=False)
        grad_all = grad_all.transpose(1, 0, 2, 3).reshape(-1, own_out)
        contract = (((0,), (0,)), ((), ()))
        outer_grad = outer_grad + lax.dot_general(
            grad_all, outer_all[part], contract, preferred_element_type=jnp.float32
        )
        high_grad = high_grad + lax.dot_general(
            grad_all, high_all[part], contract, preferred_element_type=jnp.float32
        )
    gain_rows = lax.all_gather(gain_grad, "dp", axis=0, tiled=False)
    grad_gain = jnp.sum(lax.all_gather(jnp.sum(gain_rows, axis=0), "tensor", axis=0, tiled=False), axis=0)
    grad_join = jnp.concatenate(
        [outer_grad.reshape(own_out, 2, width), high_grad[:, None]], axis=1
    )
    return (grad_join, grad_gain)


def solution(mesh):
    return jax.shard_map(
        on_device,
        mesh=mesh,
        in_specs=(
            P("dp", "tensor"),
            P("tensor", None),
            P("tensor", None),
            P("dp", "tensor"),
            P("dp", "tensor"),
            P("dp", "tensor"),
            P("dp", None, "tensor"),
            P(),
            P(None, ("dp", "tensor"), None),
            P(("dp", "tensor")),
        ),
        out_specs=(P("dp", None, "tensor"), P()),
        check_vma=False,
    )
```

profile of v0, /device:TPU:0, one launch (start us, length us, event | category | flops | bytes accessed | tf_op | source)
XLA Modules:
  0.0 485.4 jit_solution(15024596831670484599)
XLA Ops:
  9.0 9.3 %fusion = bf16[1024,4096]{1,0:T(8,128)(2,1)} fusion(bf16[1024,4096]{1,0:T(8,128)(2,1)} %param.11, f32[8,4096]{1,0:T(8,128)S(1)} %broadcast_bitcast_fusion), kind=kLoop, calls=%fused_computation.1 | loop fusion | flops 12582912 | bytes 16908288 | tf_op jit(solution)/shard_map/convert_element_type | solution.py:18
  32.6 51.5 %reduce-scatter.10.cloned.1.call-done = bf16[1,512,1024]{1,2,0:T(8,128)(2,1)} async-done(((bf16[4,512,1024]{1,2,0:T(8,128)(2,1)}), bf16[1,512,1024]{1,2,0:T(8,128)(2,1)}) %reduce-scatter.10.cloned.1.call-update) | async-done | bytes 1048592
  86.1 30.6 %all-gather.13.cloned.1.call-done = bf16[2048,2048]{1,0:T(8,128)(2,1)} async-done(((bf16[256,2048]{1,0:T(8,128)(2,1)}), bf16[2048,2048]{1,0:T(8,128)(2,1)}) %all-gather.13.cloned.1.call-update) | async-done | bytes 8388624 | tf_op jit(solution)/shard_map/all_gather | solution.py:69
  120.6 78.1 %all-gather.17.cloned.1.call-done = bf16[2048,2048]{1,0:T(8,128)(2,1)} async-done(((bf16[256,2048]{1,0:T(8,128)(2,1)}), bf16[2048,2048]{1,0:T(8,128)(2,1)}) %all-gather.17.cloned.1.call-update) | async-done | bytes 8388624 | tf_op jit(solution)/shard_map/all_gather | solution.py:69
  198.7 46.9 %all-gather.15.cloned.1.call-done = bf16[2048,1024]{1,0:T(8,128)(2,1)} async-done(((bf16[256,1024]{1,0:T(8,128)(2,1)}), bf16[2048,1024]{1,0:T(8,128)(2,1)}) %all-gather.15.cloned.1.call-update) | async-done | bytes 4194320 | tf_op jit(solution)/shard_map/all_gather | solution.py:69
  245.6 4.9 %fusion.82 = f32[2048,512]{1,0:T(8,128)S(1)} fusion(bf16[2048,1024]{1,0:T(8,128)(2,1)} %all-gather.15.cloned.1.call-done, bf16[512,3,1024]{2,0,1:T(8,128)(2,1)} %param.16), kind=kOutput, calls=%fused_computation.106 | convolution fusion | flops 2147483648 | bytes 9437184 | tf_op jit(solution)/shard_map/dot_general | solution.py:91
  250.5 8.3 %add_convert_fusion.1 = bf16[2048,512]{1,0:T(8,128)(2,1)S(1)} fusion(f32[2048,512]{1,0:T(8,128)S(1)} %fusion.82, bf16[2048,2048]{1,0:T(8,128)(2,1)} %all-gather.13.cloned.1.call-done, bf16[512,2048]{0,1:T(8,128)(2,1)S(1)} %bitcast.285), kind=kOutput, calls=%fused_computation.6 | convolution fusion | flops 4297064448 | bytes 16777216 | tf_op jit(solution)/shard_map/dot_general | solution.py:89
  262.3 33.3 %reduce-scatter.12.cloned.1.call-done = bf16[1,8,64,512]{3,1,2,0:T(8,128)(2,1)} async-done(((bf16[4,8,64,512]{3,1,2,0:T(8,128)(2,1)}), bf16[1,8,64,512]{3,1,2,0:T(8,128)(2,1)}) %reduce-scatter.12.cloned.1.call-update) | async-done | bytes 524304
  297.6 4.6 all-to-all-start
  302.4 4.4 slice_convert_fusion.2
  311.9 7.1 %all-to-all-done = bf16[8,64,512]{2,1,0:T(8,128)(2,1)S(1)} async-done(((bf16[8,64,512]{2,1,0:T(8,128)(2,1)}), bf16[8,64,512]{2,1,0:T(8,128)(2,1)S(1)}, u32[]{:S(2)}, u32[]{:S(2)}) %all-to-all-start) | async-done | bytes 524320 | tf_op jit(solution)/shard_map/all_to_all | solution.py:98
  320.7 5.0 %fusion.80 = f32[2048,512]{1,0:T(8,128)S(1)} fusion(bf16[2048,1024]{1,0:T(8,128)(2,1)} %all-gather.19.cloned.1.call-done, bf16[512,3,1024]{2,0,1:T(8,128)(2,1)} %param.16), kind=kOutput, calls=%fused_computation.104 | convolution fusion | flops 2147483648 | bytes 9437184 | tf_op jit(solution)/shard_map/dot_general | solution.py:91
  325.8 8.7 %add_convert_fusion = bf16[2048,512]{1,0:T(8,128)(2,1)S(1)} fusion(f32[2048,512]{1,0:T(8,128)S(1)} %fusion.80, bf16[2048,2048]{1,0:T(8,128)(2,1)} %all-gather.17.cloned.1.call-done, bf16[512,2048]{0,1:T(8,128)(2,1)S(1)} %bitcast.286), kind=kOutput, calls=%fused_computation.5 | convolution fusion | flops 4297064448 | bytes 16777216 | tf_op jit(solution)/shard_map/dot_general | solution.py:89
  345.8 18.6 %all_to_all.20 = bf16[8,64,512]{2,1,0:T(8,128)(2,1)} all-to-all(bf16[8,64,512]{2,1,0:T(8,128)(2,1)S(1)} %copy.74), channel_id=1, replica_groups=mesh['dp'=8,'tensor'=4] {'dp'}, dimensions={0} | all-to-all | bytes 1048576 | tf_op jit(solution)/shard_map/all_to_all | solution.py:110
  364.3 6.7 %reduce-scatter.14.cloned.1.call-done = bf16[1,8,64,512]{3,1,2,0:T(8,128)(2,1)} async-done(((bf16[4,8,64,512]{3,1,2,0:T(8,128)(2,1)}), bf16[1,8,64,512]{3,1,2,0:T(8,128)(2,1)}) %reduce-scatter.14.cloned.1.call-update) | async-done | bytes 524304
  373.0 4.6 all-to-all-start.2
  384.1 8.9 %all-to-all-done.2 = bf16[8,64,512]{2,1,0:T(8,128)(2,1)S(1)} async-done(((bf16[8,64,512]{2,1,0:T(8,128)(2,1)}), bf16[8,64,512]{2,1,0:T(8,128)(2,1)S(1)}, u32[]{:S(2)}, u32[]{:S(2)}) %all-to-all-start.2) | async-done | bytes 524320 | tf_op jit(solution)/shard_map/all_to_all | solution.py:98
  403.4 3.5 all-to-all-start.3
  407.4 14.8 %all-to-all-done.3 = bf16[8,64,512]{2,1,0:T(8,128)(2,1)S(1)} async-done(((bf16[8,64,512]{2,1,0:T(8,128)(2,1)}), bf16[8,64,512]{2,1,0:T(8,128)(2,1)S(1)}, u32[]{:S(2)}, u32[]{:S(2)}) %all-to-all-start.3) | async-done | bytes 524320 | tf_op jit(solution)/shard_map/all_to_all | solution.py:110
  428.6 6.0 %fusion.100 = f32[512,2048]{1,0:T(8,128)} fusion(bf16[2048,512]{1,0:T(8,128)(2,1)S(1)} %bitcast.289, bf16[2048,2048]{1,0:T(8,128)(2,1)S(1)} %bitcast.311), kind=kOutput, calls=%fused_computation.161 | convolution fusion | flops 4294967296 | bytes 14680064 | tf_op jit(solution)/shard_map/dot_general | solution.py:116
  434.6 14.8 %all-gather.4 = f32[8,3,4096]{2,1,0:T(4,128)S(1)} all-gather(f32[1,3,4096]{2,1,0:T(4,128)S(1)} %bitcast.296), channel_id=4, replica_groups=mesh['dp'=8,'tensor'=4] {'dp'}, dimensions={0}, use_global_device_ids=true | all-gather | bytes 442368 | tf_op jit(solution)/shard_map/all_gather | solution.py:122
  449.5 9.8 %all-gather.5 = f32[4,3,4096]{2,1,0:T(4,128)S(1)} all-gather(f32[1,3,4096]{2,1,0:T(4,128)S(1)} %bitcast.297), channel_id=5, replica_groups=mesh['dp'=8,'tensor'=4] {'tensor'}, dimensions={0}, use_global_device_ids=true | all-gather | bytes 245760 | tf_op jit(solution)/shard_map/all_gather | solution.py:123
  462.9 7.1 %convolution_add_fusion = f32[512,2048]{1,0:T(8,128)S(1)} fusion(f32[512,2048]{1,0:T(8,128)S(1)} %copy-done.4, bf16[2048,512]{1,0:T(8,128)(2,1)S(1)} %bitcast.268, bf16[2048,2048]{1,0:T(8,128)(2,1)} %all-gather.17.cloned.1.call-done), kind=kOutput, calls=%fused_computation.7 | convolution fusion | flops 4296015872 | bytes 18874368 | tf_op jit(solution)/shard_map/dot_general | solution.py:116
  474.6 3.3 pad_maximum_fusion
  (134 shorter events, 78.4 us)
Async XLA Ops:
  8.0 10.3 %copy-start = (bf16[512,1024]{1,0:T(8,128)(2,1)S(1)}, bf16[512,1024]{1,0:T(8,128)(2,1)}, u32[]{:S(2)}) copy-start(bf16[512,1024]{1,0:T(8,128)(2,1)} %param.10) | copy-start | bytes 3145732
  8.0 76.1 %reduce-scatter.10.cloned.1.call-start = ((), (), s32[]{:S(2)}) async-start(), calls=%async_computation.13 | async-start | bytes 5242880
  18.3 4.0 copy-start.3
  28.6 88.1 %all-gather.13.cloned.1.call-start = ((), (), s32[]{:S(2)}) async-start(), calls=%async_computation.7 | async-start | bytes 9437184 | tf_op jit(solution)/shard_map/all_gather | solution.py:69
  30.3 55.3 %copy-start.12 = (bf16[512,1024]{1,0:T(8,128)(2,1)S(1)}, bf16[512,1024]{1,0:T(8,128)(2,1)}, u32[]{:S(2)}) copy-start(bf16[512,1024]{1,0:T(8,128)(2,1)} %param.13) | copy-start | bytes 3145732
  32.0 166.7 %all-gather.17.cloned.1.call-start = ((), (), s32[]{:S(2)}) async-start(), calls=%async_computation.9 | async-start | bytes 9437184 | tf_op jit(solution)/shard_map/all_gather | solution.py:69
  32.6 213.0 %all-gather.15.cloned.1.call-start = ((), (), s32[]{:S(2)}) async-start(), calls=%async_computation.8 | async-start | bytes 4718592 | tf_op jit(solution)/shard_map/all_gather | solution.py:69
  86.1 32.0 %slice-start = ((bf16[512,3,1024]{2,0,1:T(8,128)(2,1)}), bf16[512,2,1024]{2,0,1:T(8,128)(2,1)S(1)}, s32[]{:S(2)}) async-start(bf16[512,3,1024]{2,0,1:T(8,128)(2,1)} %param.16), calls=%async_computation.16 | async-start | bytes 4194304 | tf_op jit(solution)/shard_map/slice | solution.py:79
  117.7 177.8 %reduce-scatter.12.cloned.1.call-start = ((), (), s32[]{:S(2)}) async-start(), calls=%async_computation.14 | async-start | bytes 2621440
  120.6 129.9 %copy-start.9 = (bf16[512,2,1024]{0,2,1:T(8,128)(2,1)S(1)}, bf16[512,2,1024]{0,2,1:T(8,128)(2,1)}, u32[]{:S(2)}) copy-start(bf16[512,2,1024]{0,2,1:T(8,128)(2,1)} %copy.82) | copy-start | bytes 6291460
  261.4 59.3 %all-gather.19.cloned.1.call-start = ((), (), s32[]{:S(2)}) async-start(), calls=%async_computation.10 | async-start | bytes 4718592 | tf_op jit(solution)/shard_map/all_gather | solution.py:69
  297.6 21.5 %all-to-all-start = ((bf16[8,64,512]{2,1,0:T(8,128)(2,1)}), bf16[8,64,512]{2,1,0:T(8,128)(2,1)S(1)}, u32[]{:S(2)}, u32[]{:S(2)}) async-start(bf16[8,64,512]{2,1,0:T(8,128)(2,1)} %copy.72), calls=%async_computation | async-start | bytes 1048576 | tf_op jit(solution)/shard_map/all_to_all | solution.py:98
  302.1 68.9 %reduce-scatter.14.cloned.1.call-start = ((), (), s32[]{:S(2)}) async-start(), calls=%async_computation.15 | async-start | bytes 2621440
  306.8 5.1 %copy-start.16 = (s32[128]{0:T(128)S(1)}, s32[128]{0:T(128)}, u32[]{:S(2)}) copy-start(s32[128]{0:T(128)} %param.19) | copy-start | bytes 1540
  320.7 5.1 %copy-start.10 = (bf16[512,2,1024]{0,2,1:T(8,128)(2,1)S(1)}, bf16[512,2,1024]{0,2,1:T(8,128)(2,1)}, u32[]{:S(2)}) copy-start(bf16[512,2,1024]{0,2,1:T(8,128)(2,1)} %copy.82) | copy-start | bytes 6291460
  337.0 5.4 %copy-start.6 = (f32[8,8,8,512]{3,2,1,0:T(8,128)S(1)}, f32[8,8,8,512]{3,2,1,0:T(8,128)}, u32[]{:S(2)}) copy-start(f32[8,8,8,512]{3,2,1,0:T(8,128)} %copy.86) | copy-start | bytes 3145732
  345.6 36.9 %copy-start.5 = (f32[1,64,4096]{2,1,0:T(8,128)S(1)}, f32[1,64,4096]{2,1,0:T(8,128)}, u32[]{:S(2)}) copy-start(f32[1,64,4096]{2,1,0:T(8,128)} %get-tuple-element.47) | copy-start | bytes 3145732
  373.0 20.0 %all-to-all-start.2 = ((bf16[8,64,512]{2,1,0:T(8,128)(2,1)}), bf16[8,64,512]{2,1,0:T(8,128)(2,1)S(1)}, u32[]{:S(2)}, u32[]{:S(2)}) async-start(bf16[8,64,512]{2,1,0:T(8,128)(2,1)} %copy.77), calls=%async_computation.2 | async-start | bytes 1048576 | tf_op jit(solution)/shard_map/all_to_all | solution.py:98
  377.6 45.4 %all-gather.21.cloned.1.call-start = ((), (), s32[]{:S(2)}) async-start(), calls=%async_computation.11 | async-start | bytes 2621440 | tf_op jit(solution)/shard_map/all_gather | solution.py:113
  384.1 12.9 %copy-start.8 = (f32[8,8,8,512]{3,2,1,0:T(8,128)S(1)}, f32[8,8,8,512]{3,2,1,0:T(8,128)}, u32[]{:S(2)}) copy-start(f32[8,8,8,512]{3,2,1,0:T(8,128)} %copy.92) | copy-start | bytes 3145732
  393.6 5.6 %copy-start.7 = (f32[8,8,8,512]{3,2,1,0:T(8,128)S(1)}, f32[8,8,8,512]{3,2,1,0:T(8,128)}, u32[]{:S(2)}) copy-start(f32[8,8,8,512]{3,2,1,0:T(8,128)} %copy.94) | copy-start | bytes 3145732
  403.4 18.8 %all-to-all-start.3 = ((bf16[8,64,512]{2,1,0:T(8,128)(2,1)}), bf16[8,64,512]{2,1,0:T(8,128)(2,1)S(1)}, u32[]{:S(2)}, u32[]{:S(2)}) async-start(bf16[8,64,512]{2,1,0:T(8,128)(2,1)} %copy.79), calls=%async_computation.3 | async-start | bytes 1048576 | tf_op jit(solution)/shard_map/all_to_all | solution.py:110
  406.9 53.2 %all-gather.23.cloned.1.call-start = ((), (), s32[]{:S(2)}) async-start(), calls=%async_computation.12 | async-start | bytes 2621440 | tf_op jit(solution)/shard_map/all_gather | solution.py:113
  423.1 5.2 %slice-start.1 = ((s8[8388608]{0:T(1024)(128)(4,1)}), s8[4194304]{0:T(1024)(128)(4,1)S(1)}, s32[]{:S(2)}) async-start(s8[8388608]{0:T(1024)(128)(4,1)} %bitcast.310), calls=%async_computation.17 | async-start | bytes 8388608
  (9 other events, 20.8 us)
Sparse Core Ops, SparseCore 0:
  28.7 55.3 reduce-scatter.9
  261.5 34.0 reduce-scatter.11
  337.1 33.8 reduce-scatter.13
  384.2 35.7 all-gather.20
  423.2 34.7 all-gather.22
Sparse Core Ops, SparseCore 1:
  32.1 84.6 all-gather.12
  118.2 80.4 all-gather.16
  200.3 45.3 all-gather.14
  263.7 47.2 all-gather.18
where the time goes:
time: 493 us; the launch traced here: 485 us
  waiting for transfers between devices  279 us (57%)
  matrix products  51.7 us (10%)
  blocking collectives  43.2 us (9%)
  local copies, waits for them, and re-layouts  40.8 us (8%)
  other arithmetic  40.3 us (8%)
  between operations  16.2 us (3%)
  starting transfers between devices  13.9 us (3%)
    all_gather x4, waiting for transfers between devices, gathered(): return lax.all_gather(own_piece, 'dp', axis=0, tiled=True)  156 us
    unnamed x12, waiting for transfers between devices  92.8 us
    unnamed x54, local copies, waits for them, and re-layouts  21.9 us
    all_to_all x1, blocking collectives, on_device(): lax.all_to_all(grad_own, 'dp', split_axis=0, concat_axis=0, tiled=True)  18.6 us
    dot_general x2, matrix products, on_device(): jnp.dot(outer_all[part], outer_weight.T, preferred_element_type=jnp.float32)  17 us
    all_to_all x2, waiting for transfers between devices, on_device(): lax.all_to_all(scattered, 'dp', split_axis=0, concat_axis=0, tiled=True)  16 us
    all_gather x1, blocking collectives, on_device(): gain_rows = lax.all_gather(gain_grad, 'dp', axis=0, tiled=False)  14.8 us
    all_to_all x1, waiting for transfers between devices, on_device(): lax.all_to_all(grad_own, 'dp', split_axis=0, concat_axis=0, tiled=True)  14.8 us
  transfers between devices with their start and end apart: 12, of which 9 were waited for; matrix products, arithmetic and copies ran while one was open for 12% of the time, Pallas kernels for 0%

commit v1 on v0

--- a/solution.py
+++ b/solution.py
@@ -68,27 +68,37 @@
     def gathered(own_piece):
         return lax.all_gather(own_piece, "dp", axis=0, tiled=True)
 
-    outer = jnp.concatenate([low_feature, mid_feature], axis=1)
-    outer_all = [gathered(piece(outer, part)) for part in range(PARTS)]
+    low_all = [gathered(piece(low_feature, part)) for part in range(PARTS)]
+    mid_all = [gathered(piece(mid_feature, part)) for part in range(PARTS)]
     partial_value = project_heads(attention, code_blocks, block_scales, n_tensor)
+    partial_value, low_all[0] = lax.optimization_barrier((partial_value, low_all[0]))
     own_share = lax.psum_scatter(partial_value, "tensor", scatter_dimension=0, tiled=False)
     high_feature = (residual.astype(jnp.float32) + own_share.astype(jnp.float32)).astype(jnp.bfloat16)
-    high_feature, outer_all[0] = lax.optimization_barrier((high_feature, outer_all[0]))
     high_all = [gathered(piece(high_feature, part)) for part in range(PARTS)]
 
-    outer_weight = join_weight[:, :2].reshape(own_out, -1)
-    high_weight = join_weight[:, 2]
+    weights = [join_weight[:, kind] for kind in range(3)]
     gain_grad = jnp.zeros(draft_gain.shape, jnp.float32)
-    outer_grad = jnp.zeros((own_out, 2 * width), jnp.float32)
-    high_grad = jnp.zeros((own_out, width), jnp.float32)
-    joined_own = grad_own = None
-    high_all[0], *outer_all = lax.optimization_barrier((high_all[0], *outer_all))
+    kind_grads = [jnp.zeros((own_out, width), jnp.float32) for _ in weights]
+    joined_own = grad_own = grad_all = None
+    high_all[0], *low_all = lax.optimization_barrier((high_all[0], *low_all))
+
+    def products(totals, grad_all, part):
+        features = (low_all[part], mid_all[part], high_all[part])
+        contract = (((0,), (0,)), ((), ()))
+        return [
+            total
+            + lax.dot_general(grad_all, feature, contract, preferred_element_type=jnp.float32)
+            for total, feature in zip(totals, features)
+        ]
+
     for part in range(PARTS):
         if part > 0:
             high_all[part], joined_own = lax.optimization_barrier((high_all[part], joined_own))
-        joined_partial = jnp.dot(
-            outer_all[part], outer_weight.T, preferred_element_type=jnp.float32
-        ) + jnp.dot(high_all[part], high_weight.T, preferred_element_type=jnp.float32)
+        features = (low_all[part], mid_all[part], high_all[part])
+        joined_partial = sum(
+            jnp.dot(feature, weight.T, preferred_element_type=jnp.float32)
+            for feature, weight in zip(features, weights)
+        )
         joined_partial = joined_partial.astype(jnp.bfloat16).reshape(n_dp, n_tensor, rows, own_out)
         scattered = lax.psum_scatter(
             joined_partial.transpose(1, 0, 2, 3), "tensor", scatter_dimension=0, tiled=False
@@ -107,23 +117,18 @@
         )
         gain_grad = gain_grad + part_gain
         grad_own = joined_grad.astype(jnp.bfloat16).reshape(rows, n_dp, own_out).transpose(1, 0, 2)
+        if part > 0:
+            grad_own, grad_all = lax.optimization_barrier((grad_own, grad_all))
+            kind_grads = products(kind_grads, grad_all, part - 1)
         grad_own = lax.all_to_all(grad_own, "dp", split_axis=0, concat_axis=0, tiled=True)
         if part == PARTS - 1:
             gain_grad, grad_own = lax.optimization_barrier((gain_grad, grad_own))
         grad_all = lax.all_gather(grad_own, "tensor", axis=0, tiled=False)
         grad_all = grad_all.transpose(1, 0, 2, 3).reshape(-1, own_out)
-        contract = (((0,), (0,)), ((), ()))
-        outer_grad = outer_grad + lax.dot_general(
-            grad_all, outer_all[part], contract, preferred_element_type=jnp.float32
-        )
-        high_grad = high_grad + lax.dot_general(
-            grad_all, high_all[part], contract, preferred_element_type=jnp.float32
-        )
+    kind_grads = products(kind_grads, grad_all, PARTS - 1)
     gain_rows = lax.all_gather(gain_grad, "dp", axis=0, tiled=False)
     grad_gain = jnp.sum(lax.all_gather(jnp.sum(gain_rows, axis=0), "tensor", axis=0, tiled=False), axis=0)
-    grad_join = jnp.concatenate(
-        [outer_grad.reshape(own_out, 2, width), high_grad[:, None]], axis=1
-    )
+    grad_join = jnp.stack(kind_grads, axis=1)
     return (grad_join, grad_gain)
 
 

time: 493 us -> 592 us (1.20)
  waiting for transfers between devices: 279 us -> 371 us
  matrix products: 51.7 us -> 65.5 us
    all_gather x4 -> x6, waiting for transfers between devices: 156 us -> 246 us  [gathered(): return lax.all_gather(own_piece, 'dp', axis=0, tiled=True)]
    all_gather x2, waiting for transfers between devices: 0.02 us -> 24 us  [on_device(): grad_all = lax.all_gather(grad_own, 'tensor', axis=0, tiled=False)]
    all_to_all x2, waiting for transfers between devices: 16 us -> 0.01 us  [on_device(): lax.all_to_all(scattered, 'dp', split_axis=0, concat_axis=0, tiled=True)]
    dot_general x8 -> x12, matrix products: 44.8 us -> 58.2 us  [the longest x6 36 us: on_device(): jnp.dot(feature, weight.T, preferred_element_type=jnp.float32)]
    unnamed x54 -> x59, local copies, waits for them, and re-layouts: 21.9 us -> 14.2 us
    unnamed x12 -> x14, waiting for transfers between devices: 92.8 us -> 86.6 us
  transfers between devices with their start and end apart: 12 -> 14, of which waited for: 9 -> 11; matrix products, arithmetic and copies ran while one was open for 12% -> 15% of each run, Pallas kernels for 0% -> 0%
where the time goes in v1:
time: 592 us; the launch traced here: 584 us
  waiting for transfers between devices  371 us (63%)
  matrix products  65.5 us (11%)
  blocking collectives  42.5 us (7%)
  other arithmetic  39.6 us (7%)
  local copies, waits for them, and re-layouts  35.7 us (6%)
  starting transfers between devices  15.4 us (3%)
  between operations  14.8 us (2%)
    all_gather x6, waiting for transfers between devices, gathered(): return lax.all_gather(own_piece, 'dp', axis=0, tiled=True)  246 us
    unnamed x14, waiting for transfers between devices  86.6 us
    dot_general x6, matrix products, on_device(): jnp.dot(feature, weight.T, preferred_element_type=jnp.float32)  36 us
    all_gather x2, waiting for transfers between devices, on_device(): grad_all = lax.all_gather(grad_own, 'tensor', axis=0, tiled=False)  24 us
    dot_general x6, matrix products, products(): lax.dot_general(grad_all, feature, contract, preferred_element_type=jnp.f...  22.2 us
    all_to_all x1, blocking collectives, on_device(): lax.all_to_all(grad_own, 'dp', split_axis=0, concat_axis=0, tiled=True)  18.6 us
    all_gather x1, blocking collectives, on_device(): gain_rows = lax.all_gather(gain_grad, 'dp', axis=0, tiled=False)  14.9 us
    all_to_all x1, waiting for transfers between devices, on_device(): lax.all_to_all(grad_own, 'dp', split_axis=0, concat_axis=0, tiled=True)  14.8 us
  transfers between devices with their start and end apart: 14, of which 11 were waited for; matrix products, arithmetic and copies ran while one was open for 15% of the time, Pallas kernels for 0%

profile of v1, /device:TPU:0, one launch (start us, length us, event | category | flops | bytes accessed | tf_op | source)
XLA Modules:
  0.0 584.4 jit_solution(6376327353401236901)
XLA Ops:
  10.5 9.3 %fusion = bf16[1024,4096]{1,0:T(8,128)(2,1)} fusion(bf16[1024,4096]{1,0:T(8,128)(2,1)} %param.11, f32[8,4096]{1,0:T(8,128)S(1)} %broadcast_bitcast_fusion), kind=kLoop, calls=%fused_computation.1 | loop fusion | flops 12582912 | bytes 16908288 | tf_op jit(solution)/shard_map/convert_element_type | solution.py:18
  30.5 29.1 %all-gather.15.cloned.1.call-done = bf16[2048,1024]{1,0:T(8,128)(2,1)} async-done(((bf16[256,1024]{1,0:T(8,128)(2,1)}), bf16[2048,1024]{1,0:T(8,128)(2,1)}) %all-gather.15.cloned.1.call-update) | async-done | bytes 4194320 | tf_op jit(solution)/shard_map/all_gather | solution.py:69
  61.4 53.2 %reduce-scatter.10.cloned.1.call-done = bf16[1,512,1024]{1,2,0:T(8,128)(2,1)} async-done(((bf16[4,512,1024]{1,2,0:T(8,128)(2,1)}), bf16[1,512,1024]{1,2,0:T(8,128)(2,1)}) %reduce-scatter.10.cloned.1.call-update) | async-done | bytes 1048592
  118.1 45.3 %all-gather.25.cloned.1.call-done = bf16[2048,1024]{1,0:T(8,128)(2,1)} async-done(((bf16[256,1024]{1,0:T(8,128)(2,1)}), bf16[2048,1024]{1,0:T(8,128)(2,1)}) %all-gather.25.cloned.1.call-update) | async-done | bytes 4194320 | tf_op jit(solution)/shard_map/all_gather | solution.py:69
  163.5 6.9 %fusion.82 = f32[2048,512]{1,0:T(8,128)} fusion(bf16[2048,1024]{1,0:T(8,128)(2,1)} %all-gather.25.cloned.1.call-done, bf16[512,3,1024]{2,0,1:T(8,128)(2,1)} %param.16), kind=kOutput, calls=%fused_computation.105 | convolution fusion | flops 2147483648 | bytes 9437184 | tf_op jit(solution)/shard_map/dot_general | solution.py:99
  170.3 40.6 %all-gather.19.cloned.1.call-done = bf16[2048,1024]{1,0:T(8,128)(2,1)} async-done(((bf16[256,1024]{1,0:T(8,128)(2,1)}), bf16[2048,1024]{1,0:T(8,128)(2,1)}) %all-gather.19.cloned.1.call-update) | async-done | bytes 4194320 | tf_op jit(solution)/shard_map/all_gather | solution.py:69
  210.9 47.4 %all-gather.17.cloned.1.call-done = bf16[2048,1024]{1,0:T(8,128)(2,1)} async-done(((bf16[256,1024]{1,0:T(8,128)(2,1)}), bf16[2048,1024]{1,0:T(8,128)(2,1)}) %all-gather.17.cloned.1.call-update) | async-done | bytes 4194320 | tf_op jit(solution)/shard_map/all_gather | solution.py:69
  258.3 5.0 fusion.86
  279.4 24.6 %reduce-scatter.12.cloned.1.call-done = bf16[1,8,64,512]{3,1,2,0:T(8,128)(2,1)} async-done(((bf16[4,8,64,512]{3,1,2,0:T(8,128)(2,1)}), bf16[1,8,64,512]{3,1,2,0:T(8,128)(2,1)}) %reduce-scatter.12.cloned.1.call-update) | async-done | bytes 524304
  306.0 4.6 all-to-all-start
  310.8 50.7 %all-gather.21.cloned.1.call-done = bf16[2048,1024]{1,0:T(8,128)(2,1)} async-done(((bf16[256,1024]{1,0:T(8,128)(2,1)}), bf16[2048,1024]{1,0:T(8,128)(2,1)}) %all-gather.21.cloned.1.call-update) | async-done | bytes 4194320 | tf_op jit(solution)/shard_map/all_gather | solution.py:69
  361.5 7.0 %fusion.84 = f32[2048,512]{1,0:T(8,128)} fusion(bf16[2048,1024]{1,0:T(8,128)(2,1)} %all-gather.21.cloned.1.call-done, bf16[512,3,1024]{2,0,1:T(8,128)(2,1)} %param.16), kind=kOutput, calls=%fused_computation.107 | convolution fusion | flops 2147483648 | bytes 9437184 | tf_op jit(solution)/shard_map/dot_general | solution.py:99
  368.5 5.7 fusion.88
  375.9 32.3 %all-gather.23.cloned.1.call-done = bf16[2048,1024]{1,0:T(8,128)(2,1)} async-done(((bf16[256,1024]{1,0:T(8,128)(2,1)}), bf16[2048,1024]{1,0:T(8,128)(2,1)}) %all-gather.23.cloned.1.call-update) | async-done | bytes 4194320 | tf_op jit(solution)/shard_map/all_gather | solution.py:69
  408.2 7.4 %add_convert_fusion = bf16[2048,512]{1,0:T(8,128)(2,1)S(1)} fusion(f32[2048,512]{1,0:T(8,128)} %fusion.88, f32[2048,512]{1,0:T(8,128)} %fusion.84, bf16[2048,1024]{1,0:T(8,128)(2,1)} %all-gather.23.cloned.1.call-done, bf16[512,3,1024]{2,0,1:T(8,128)(2,1)} %param.16), kind=kOutput, calls=%fused_computation.4 | convolution fusion | flops 2150629376 | bytes 15728640 | tf_op jit(solution)/shard_map/dot_general | solution.py:99
  426.9 18.6 %all_to_all.20 = bf16[8,64,512]{2,1,0:T(8,128)(2,1)} all-to-all(bf16[8,64,512]{2,1,0:T(8,128)(2,1)S(1)} %copy.65), channel_id=1, replica_groups=mesh['dp'=8,'tensor'=4] {'dp'}, dimensions={0} | all-to-all | bytes 1048576 | tf_op jit(solution)/shard_map/all_to_all | solution.py:123
  445.5 6.7 %reduce-scatter.14.cloned.1.call-done = bf16[1,8,64,512]{3,1,2,0:T(8,128)(2,1)} async-done(((bf16[4,8,64,512]{3,1,2,0:T(8,128)(2,1)}), bf16[1,8,64,512]{3,1,2,0:T(8,128)(2,1)}) %reduce-scatter.14.cloned.1.call-update) | async-done | bytes 524304
  454.2 4.8 all-to-all-start.2
  465.3 24.0 %all-gather.27.cloned.1.call-done = bf16[32,64,512]{2,1,0:T(8,128)(2,1)} async-done(((bf16[8,64,512]{2,1,0:T(8,128)(2,1)}), bf16[32,64,512]{2,1,0:T(8,128)(2,1)}) %all-gather.27.cloned.1.call-update) | async-done | bytes 2097168 | tf_op jit(solution)/shard_map/all_gather | solution.py:126
  503.0 4.6 all-to-all-start.3
  508.2 14.8 %all-to-all-done.3 = bf16[8,64,512]{2,1,0:T(8,128)(2,1)S(1)} async-done(((bf16[8,64,512]{2,1,0:T(8,128)(2,1)}), bf16[8,64,512]{2,1,0:T(8,128)(2,1)S(1)}, u32[]{:S(2)}, u32[]{:S(2)}) %all-to-all-start.3) | async-done | bytes 524320 | tf_op jit(solution)/shard_map/all_to_all | solution.py:123
  523.8 6.1 %fusion.111 = f32[512,1024]{1,0:T(8,128)} fusion(bf16[2048,512]{1,0:T(8,128)(2,1)S(1)} %bitcast.296, bf16[2048,1024]{1,0:T(8,128)(2,1)} %all-gather.15.cloned.1.call-done), kind=kOutput, calls=%fused_computation.171 | convolution fusion | flops 2147483648 | bytes 8388608 | tf_op jit(solution)/shard_map/dot_general | solution.py:90
  537.3 14.9 %all-gather.4 = f32[8,3,4096]{2,1,0:T(4,128)S(1)} all-gather(f32[1,3,4096]{2,1,0:T(4,128)S(1)} %bitcast.313), channel_id=4, replica_groups=mesh['dp'=8,'tensor'=4] {'dp'}, dimensions={0}, use_global_device_ids=true | all-gather | bytes 442368 | tf_op jit(solution)/shard_map/all_gather | solution.py:129
  552.3 9.0 %all-gather.5 = f32[4,3,4096]{2,1,0:T(4,128)S(1)} all-gather(f32[1,3,4096]{2,1,0:T(4,128)S(1)} %bitcast.314), channel_id=5, replica_groups=mesh['dp'=8,'tensor'=4] {'tensor'}, dimensions={0}, use_global_device_ids=true | all-gather | bytes 245760 | tf_op jit(solution)/shard_map/all_gather | solution.py:130
  (145 shorter events, 96.7 us)
Async XLA Ops:
  7.2 12.7 %copy-start = (bf16[512,1024]{1,0:T(8,128)(2,1)S(1)}, bf16[512,1024]{1,0:T(8,128)(2,1)}, u32[]{:S(2)}) copy-start(bf16[512,1024]{1,0:T(8,128)(2,1)} %param.10) | copy-start | bytes 3145732
  7.2 52.4 %all-gather.15.cloned.1.call-start = ((), (), s32[]{:S(2)}) async-start(), calls=%async_computation.7 | async-start | bytes 4718592 | tf_op jit(solution)/shard_map/all_gather | solution.py:69
  9.6 105.0 %reduce-scatter.10.cloned.1.call-start = ((), (), s32[]{:S(2)}) async-start(), calls=%async_computation.15 | async-start | bytes 5242880
  30.5 29.2 %copy-start.16 = (bf16[512,1024]{1,0:T(8,128)(2,1)S(1)}, bf16[512,1024]{1,0:T(8,128)(2,1)}, u32[]{:S(2)}) copy-start(bf16[512,1024]{1,0:T(8,128)(2,1)} %param.15) | copy-start | bytes 3145732
  30.5 85.6 %copy-start.15 = (bf16[512,1024]{1,0:T(8,128)(2,1)S(1)}, bf16[512,1024]{1,0:T(8,128)(2,1)}, u32[]{:S(2)}) copy-start(bf16[512,1024]{1,0:T(8,128)(2,1)} %param.13) | copy-start | bytes 3145732
  59.6 103.8 %all-gather.25.cloned.1.call-start = ((), (), s32[]{:S(2)}) async-start(), calls=%async_computation.12 | async-start | bytes 4718592 | tf_op jit(solution)/shard_map/all_gather | solution.py:69
  60.8 150.1 %all-gather.19.cloned.1.call-start = ((), (), s32[]{:S(2)}) async-start(), calls=%async_computation.9 | async-start | bytes 4718592 | tf_op jit(solution)/shard_map/all_gather | solution.py:69
  61.4 197.0 %all-gather.17.cloned.1.call-start = ((), (), s32[]{:S(2)}) async-start(), calls=%async_computation.8 | async-start | bytes 4718592 | tf_op jit(solution)/shard_map/all_gather | solution.py:69
  117.6 186.4 %reduce-scatter.12.cloned.1.call-start = ((), (), s32[]{:S(2)}) async-start(), calls=%async_computation.16 | async-start | bytes 2621440
  269.9 91.6 %all-gather.21.cloned.1.call-start = ((), (), s32[]{:S(2)}) async-start(), calls=%async_computation.10 | async-start | bytes 4718592 | tf_op jit(solution)/shard_map/all_gather | solution.py:69
  270.7 137.5 %all-gather.23.cloned.1.call-start = ((), (), s32[]{:S(2)}) async-start(), calls=%async_computation.11 | async-start | bytes 4718592 | tf_op jit(solution)/shard_map/all_gather | solution.py:69
  306.0 68.3 %all-to-all-start = ((bf16[8,64,512]{2,1,0:T(8,128)(2,1)}), bf16[8,64,512]{2,1,0:T(8,128)(2,1)S(1)}, u32[]{:S(2)}, u32[]{:S(2)}) async-start(bf16[8,64,512]{2,1,0:T(8,128)(2,1)} %copy.62), calls=%async_computation | async-start | bytes 1048576 | tf_op jit(solution)/shard_map/all_to_all | solution.py:108
  310.6 141.6 %reduce-scatter.14.cloned.1.call-start = ((), (), s32[]{:S(2)}) async-start(), calls=%async_computation.17 | async-start | bytes 2621440
  361.5 7.0 %copy-start.2 = (bf16[2048,1024]{1,0:T(8,128)(2,1)S(1)}, bf16[2048,1024]{1,0:T(8,128)(2,1)}, u32[]{:S(2)}) copy-start(bf16[2048,1024]{1,0:T(8,128)(2,1)} %all-gather.19.cloned.1.call-done) | copy-start | bytes 12582916
  418.1 71.3 %all-gather.27.cloned.1.call-start = ((), (), s32[]{:S(2)}) async-start(), calls=%async_computation.13 | async-start | bytes 2621440 | tf_op jit(solution)/shard_map/all_gather | solution.py:126
  426.9 36.9 %copy-start.7 = (f32[1,64,4096]{2,1,0:T(8,128)S(1)}, f32[1,64,4096]{2,1,0:T(8,128)}, u32[]{:S(2)}) copy-start(f32[1,64,4096]{2,1,0:T(8,128)} %get-tuple-element.51) | copy-start | bytes 3145732
  454.2 38.4 %all-to-all-start.2 = ((bf16[8,64,512]{2,1,0:T(8,128)(2,1)}), bf16[8,64,512]{2,1,0:T(8,128)(2,1)S(1)}, u32[]{:S(2)}, u32[]{:S(2)}) async-start(bf16[8,64,512]{2,1,0:T(8,128)(2,1)} %copy.66), calls=%async_computation.2 | async-start | bytes 1048576 | tf_op jit(solution)/shard_map/all_to_all | solution.py:108
  489.4 7.2 %copy-start.10 = (f32[8,8,8,512]{3,2,1,0:T(8,128)S(1)}, f32[8,8,8,512]{3,2,1,0:T(8,128)}, u32[]{:S(2)}) copy-start(f32[8,8,8,512]{3,2,1,0:T(8,128)} %copy.75) | copy-start | bytes 3145732
  493.2 5.6 copy-start.9
  498.8 25.0 %copy-start.11 = (bf16[8,4,64,512]{3,2,1,0:T(8,128)(2,1)S(1)}, bf16[8,4,64,512]{3,2,1,0:T(8,128)(2,1)}, u32[]{:S(2)}) copy-start(bf16[8,4,64,512]{3,2,1,0:T(8,128)(2,1)} %copy.68) | copy-start | bytes 6291460
  503.0 20.0 %all-to-all-start.3 = ((bf16[8,64,512]{2,1,0:T(8,128)(2,1)}), bf16[8,64,512]{2,1,0:T(8,128)(2,1)S(1)}, u32[]{:S(2)}, u32[]{:S(2)}) async-start(bf16[8,64,512]{2,1,0:T(8,128)(2,1)} %copy.69), calls=%async_computation.3 | async-start | bytes 1048576 | tf_op jit(solution)/shard_map/all_to_all | solution.py:123
  507.6 54.4 %all-gather.29.cloned.1.call-start = ((), (), s32[]{:S(2)}) async-start(), calls=%async_computation.14 | async-start | bytes 2621440 | tf_op jit(solution)/shard_map/all_gather | solution.py:126
  523.8 6.1 %copy-start.21 = (bf16[2048,1024]{1,0:T(8,128)(2,1)S(1)}, bf16[2048,1024]{1,0:T(8,128)(2,1)}, u32[]{:S(2)}) copy-start(bf16[2048,1024]{1,0:T(8,128)(2,1)} %all-gather.17.cloned.1.call-done) | copy-start | bytes 12582916
  571.8 5.6 copy-start.1
  (13 other events, 48.5 us)
Sparse Core Ops, SparseCore 0:
  9.7 49.8 all-gather.14
  63.1 51.4 reduce-scatter.9
  116.3 47.1 all-gather.24
  165.0 45.8 all-gather.18
  212.4 45.8 all-gather.16
  270.0 33.8 reduce-scatter.11
  305.6 55.9 all-gather.20
  363.1 44.9 all-gather.22
  418.2 33.9 reduce-scatter.13
  454.0 35.3 all-gather.26
  523.9 33.4 all-gather.28
